TPU v7x, 32 devices: a whole 2x2x4 slice. The times are simulated.
32 devices in a mesh: dp: 16 (over z, y, x), tensor: 2 (over core).
Axes of the slice: x: 2, y: 2, z: 4, core: 2. Of those that a mesh axis runs over, the one named last changes fastest.
Arguments:
- decoder_input: bfloat16 [16, 1024, 512], P('dp'), may hold values from -6 to 6
- encoder_states: bfloat16 [16, 1024, 512], P('dp'), may hold values from -6 to 6
- decoder_segments: int32 [16, 1024], P('dp'), may hold values from 0 to 3, never falling along the last dimension, each value on 1 to 512 neighbouring positions
- encoder_segments: int32 [16, 1024], P('dp'), may hold values from 0 to 3, never falling along the last dimension, each value on 1 to 512 neighbouring positions
- output_cotangent: bfloat16 [16, 1024, 512], P('dp'), may hold values from -6 to 6
- block_slots: int32 [256], replicated, may hold values from 0 to 255, as said below
- master: float32 [2, 256, 128, 64], P('tensor', 'dp')
- first_moment: float32 [2, 256, 128, 64], P('tensor', 'dp')
- second_moment: float32 [2, 256, 128, 64], P('tensor', 'dp'), as said below
- row_statistics: float32 [2, 256, 128, 128], P('tensor', 'dp')
- column_statistics: float32 [2, 256, 64, 64], P('tensor', 'dp')
- row_basis: float32 [2, 256, 128, 128], P('tensor', 'dp')
- column_basis: float32 [2, 256, 64, 64], P('tensor', 'dp')
- vectors: float32 [6, 512], P(None, 'dp')
- vector_first: float32 [6, 512], P(None, 'dp')
- vector_second: float32 [6, 512], P(None, 'dp'), as said below
Outputs:
- block_output: bfloat16 [16, 1024, 512], P('dp')
- input_gradient: float32 [16, 1024, 512], P('dp')
- encoder_gradient: float32 [16, 1024, 512], P('dp')
- new_master: float32 [2, 256, 128, 64], P('tensor', 'dp')
- new_first_moment: float32 [2, 256, 128, 64], P('tensor', 'dp')
- new_second_moment: float32 [2, 256, 128, 64], P('tensor', 'dp')
- new_row_statistics: float32 [2, 256, 128, 128], P('tensor', 'dp')
- new_column_statistics: float32 [2, 256, 64, 64], P('tensor', 'dp')
- new_row_basis: float32 [2, 256, 128, 128], P('tensor', 'dp')
- new_column_basis: float32 [2, 256, 64, 64], P('tensor', 'dp')
- new_vectors: float32 [6, 512], P(None, 'dp')
- new_vector_first: float32 [6, 512], P(None, 'dp')
- new_vector_second: float32 [6, 512], P(None, 'dp')
Inputs may be any that keep to these rules, and one draw needn't show every extreme that they name: `block_slots`: each number appears exactly once. `decoder_segments`: within a sequence the numbers never fall; each of the 4 documents has 1 to 512 tokens, one exactly that many. `encoder_segments`: within a sequence the numbers never fall; each of the 4 documents has 1 to 512 positions, one exactly that many. `second_moment`: every entry is positive. `vector_second`: every entry is positive.
All inputs are finite; a program needn't handle non-finite values.
Results may differ from a plain program's by a relative error of at most 0.029.
Values may be sent and summed in bfloat16 or wider, within the bound.
No kernel may reach another device: no remote copies, remote signals or barrier semaphores. Data moves between devices by JAX's collectives and lax.ppermute only.
A program may use at most 128 MiB of HBM per device.

v0:
```python
import jax
import jax.numpy as jnp
from jax import lax
from jax.sharding import PartitionSpec as P

HD = 64
FF = 2048
STEP = 10


PRECISE = lax.Precision.HIGHEST
NEGATIVE = -1e30
EPS_NORM = 1e-05
MOMENT_DECAY = 0.5
LEARN_RATE = 0.04
WEIGHT_DECAY = 0.01
VECTOR_RATE = 0.25
ADAM_EPS = 1e-08
newton_turns = 8


def layer_norm(inputs, gain, shift):
    center = inputs - jnp.mean(inputs, axis=-1, keepdims=True)
    spread = jnp.mean(center * center, axis=-1, keepdims=True)
    return center * lax.rsqrt(spread + EPS_NORM) * gain + shift


def project(inputs, matrix):
    return jnp.dot(inputs, matrix, preferred_element_type=jnp.float32).astype(jnp.bfloat16)


def times_transposed(left, right):
    return lax.dot_general(
        left, right, (((1,), (1,)), ((), ())), preferred_element_type=jnp.float32
    )


def transposed_times(left, right):
    return lax.dot_general(
        left, right, (((0,), (0,)), ((), ())), preferred_element_type=jnp.float32
    )


def branch_sum(partial_value):
    return lax.psum(partial_value.astype(jnp.bfloat16), "tensor").astype(jnp.float32)


def gradient_sum(partial_value):
    return lax.psum(partial_value.astype(jnp.bfloat16), "tensor").astype(jnp.float32)


def allowed_keys(query_segments, key_segments, offset, causal):
    allowed = query_segments[:, None] == key_segments[None, :]
    if causal:
        query_places = offset + jnp.arange(query_segments.shape[0])
        allowed = allowed & (jnp.arange(key_segments.shape[0])[None, :] <= query_places[:, None])
    return allowed


def attend_forward(queries, key_rows, values, query_segments, key_segments, causal):
    length = queries.shape[0]
    key_count = key_rows.shape[0]
    head_count = queries.shape[1] // HD
    block_rows = min(512, length)
    factor = HD ** (-0.5)
    key_heads = key_rows.reshape(key_count, head_count, HD)
    value_heads = values.reshape(key_count, head_count, HD)

    def one_block(number):
        offset = number * block_rows
        query_heads = lax.dynamic_slice_in_dim(queries, offset, block_rows, 0).reshape(
            block_rows, head_count, HD
        )
        allowed = allowed_keys(
            lax.dynamic_slice_in_dim(query_segments, offset, block_rows, 0),
            key_segments,
            offset,
            causal,
        )
        scores = (
            jnp.einsum("qhe,khe->hqk", query_heads, key_heads, preferred_element_type=jnp.float32)
            * factor
        )
        scores = jnp.where(allowed[None], scores, NEGATIVE)
        highest = jnp.max(scores, axis=-1, keepdims=True)
        expons = jnp.exp(scores - highest)
        denominator = jnp.sum(expons, axis=-1, keepdims=True)
        chances = (expons / denominator).astype(jnp.bfloat16)
        context = jnp.einsum(
            "hqk,khe->qhe", chances, value_heads, preferred_element_type=jnp.float32
        )
        return (
            context.reshape(block_rows, head_count * HD),
            (highest + jnp.log(denominator))[:, :, 0],
        )

    context, logsum = lax.map(one_block, jnp.arange(length // block_rows))
    return (
        context.reshape(length, head_count * HD),
        logsum.transpose(1, 0, 2).reshape(head_count, length),
    )


def attend_backward(
    queries, key_rows, values, logsum, grad_context, query_segments, key_segments, causal
):
    length = queries.shape[0]
    key_count = key_rows.shape[0]
    head_count = queries.shape[1] // HD
    block_rows = min(512, length)
    factor = HD ** (-0.5)
    key_heads = key_rows.reshape(key_count, head_count, HD)
    value_heads = values.reshape(key_count, head_count, HD)

    def one_block(running, number):
        grad_keys, grad_values = running
        offset = number * block_rows
        query_heads = lax.dynamic_slice_in_dim(queries, offset, block_rows, 0).reshape(
            block_rows, head_count, HD
        )
        grad_heads = lax.dynamic_slice_in_dim(grad_context, offset, block_rows, 0).reshape(
            block_rows, head_count, HD
        )
        allowed = allowed_keys(
            lax.dynamic_slice_in_dim(query_segments, offset, block_rows, 0),
            key_segments,
            offset,
            causal,
        )
        scores = (
            jnp.einsum("qhe,khe->hqk", query_heads, key_heads, preferred_element_type=jnp.float32)
            * factor
        )
        scores = jnp.where(allowed[None], scores, NEGATIVE)
        chances = jnp.exp(
            scores - lax.dynamic_slice_in_dim(logsum, offset, block_rows, 1)[:, :, None]
        )
        grad_chances = jnp.einsum(
            "qhe,khe->hqk", grad_heads, value_heads, preferred_element_type=jnp.float32
        )
        grad_values = grad_values + jnp.einsum(
            "hqk,qhe->khe",
            chances.astype(jnp.bfloat16),
            grad_heads,
            preferred_element_type=jnp.float32,
        )
        grad_scores = chances * (
            grad_chances - jnp.sum(grad_chances * chances, axis=-1, keepdims=True)
        )
        grad_scores = grad_scores.astype(jnp.bfloat16)
        grad_query = (
            jnp.einsum("hqk,khe->qhe", grad_scores, key_heads, preferred_element_type=jnp.float32)
            * factor
        )
        grad_keys = (
            grad_keys
            + jnp.einsum(
                "hqk,qhe->khe", grad_scores, query_heads, preferred_element_type=jnp.float32
            )
            * factor
        )
        return ((grad_keys, grad_values), grad_query.reshape(block_rows, head_count * HD))

    zeros = jnp.zeros((key_count, head_count, HD), jnp.float32)
    sums, grad_query = lax.scan(one_block, (zeros, zeros), jnp.arange(length // block_rows))
    return (
        grad_query.reshape(length, head_count * HD),
        sums[0].reshape(key_count, head_count * HD),
        sums[1].reshape(key_count, head_count * HD),
    )


def attend_sequences(queries, key_rows, values, query_segments, key_segments, causal):
    seq_count = query_segments.shape[0]
    columns = queries.shape[1]

    def attend_one_sequence(items):
        return attend_forward(items[0], items[1], items[2], items[3], items[4], causal)

    context, logsum = lax.map(
        attend_one_sequence,
        (
            queries.reshape(seq_count, -1, columns),
            key_rows.reshape(seq_count, -1, columns),
            values.reshape(seq_count, -1, columns),
            query_segments,
            key_segments,
        ),
    )
    return (context.reshape(-1, columns), logsum)


def back_sequences(
    queries, key_rows, values, logsum, grad_context, query_segments, key_segments, causal
):
    seq_count = query_segments.shape[0]
    columns = queries.shape[1]

    def back_one_sequence(items):
        return attend_backward(
            items[0], items[1], items[2], items[3], items[4], items[5], items[6], causal
        )

    grad_query, grad_keys, grad_values = lax.map(
        back_one_sequence,
        (
            queries.reshape(seq_count, -1, columns),
            key_rows.reshape(seq_count, -1, columns),
            values.reshape(seq_count, -1, columns),
            logsum,
            grad_context.reshape(seq_count, -1, columns),
            query_segments,
            key_segments,
        ),
    )
    return (
        grad_query.reshape(-1, columns),
        grad_keys.reshape(-1, columns),
        grad_values.reshape(-1, columns),
    )


def weight_runs(weights):
    hidden_width = FF // lax.axis_size("tensor")
    head_width = (weights.shape[1] - 2 * hidden_width) // 8
    runs = [weights[:, number * head_width : (number + 1) * head_width] for number in range(8)]
    runs.append(weights[:, 8 * head_width : 8 * head_width + hidden_width])
    runs.append(weights[:, 8 * head_width + hidden_width :])
    return runs


def forward(
    decoder_input, encoder_states, decoder_segments, encoder_segments, weights, vector_rows
):
    width = decoder_input.shape[2]
    runs = weight_runs(weights)
    tokens = decoder_input.reshape(-1, width)
    encoder_rows = encoder_states.reshape(-1, width)
    self_query = project(tokens, runs[0])
    self_key = project(tokens, runs[1])
    self_value = project(tokens, runs[2])
    self_context, self_logsum = attend_sequences(
        self_query, self_key, self_value, decoder_segments, decoder_segments, True
    )
    self_context = self_context.astype(jnp.bfloat16)
    resid_one = tokens.astype(jnp.float32) + branch_sum(times_transposed(self_context, runs[3]))
    normed_one = layer_norm(resid_one, vector_rows[0], vector_rows[1])
    normed_one_low = normed_one.astype(jnp.bfloat16)
    cross_query = project(normed_one_low, runs[4])
    cross_key = project(encoder_rows, runs[5])
    cross_value = project(encoder_rows, runs[6])
    cross_context, cross_logsum = attend_sequences(
        cross_query, cross_key, cross_value, decoder_segments, encoder_segments, False
    )
    cross_context = cross_context.astype(jnp.bfloat16)
    resid_two = normed_one + branch_sum(times_transposed(cross_context, runs[7]))
    normed_two = layer_norm(resid_two, vector_rows[2], vector_rows[3])
    normed_two_low = normed_two.astype(jnp.bfloat16)
    up_values = jnp.dot(normed_two_low, runs[8], preferred_element_type=jnp.float32)
    hidden = jax.nn.gelu(up_values).astype(jnp.bfloat16)
    resid_three = normed_two + branch_sum(times_transposed(hidden, runs[9]))
    output = layer_norm(resid_three, vector_rows[4], vector_rows[5])
    return {
        "tokens": tokens,
        "encoder_rows": encoder_rows,
        "self_query": self_query,
        "self_key": self_key,
        "self_value": self_value,
        "self_context": self_context,
        "self_logsum": self_logsum,
        "resid_one": resid_one,
        "normed_one_low": normed_one_low,
        "cross_query": cross_query,
        "cross_key": cross_key,
        "cross_value": cross_value,
        "cross_context": cross_context,
        "cross_logsum": cross_logsum,
        "resid_two": resid_two,
        "normed_two_low": normed_two_low,
        "up_values": up_values,
        "hidden": hidden,
        "resid_three": resid_three,
        "output": output,
    }


def attention_back(
    grad_branch,
    context,
    queries,
    key_rows,
    values,
    logsum,
    query_segments,
    key_segments,
    causal,
    out_matrix,
):
    grad_low = grad_branch.astype(jnp.bfloat16)
    grad_out_matrix = transposed_times(grad_low, context)
    grad_context = jnp.dot(grad_low, out_matrix, preferred_element_type=jnp.float32).astype(
        jnp.bfloat16
    )
    grad_query, grad_keys, grad_values = back_sequences(
        queries, key_rows, values, logsum, grad_context, query_segments, key_segments, causal
    )
    return (
        grad_out_matrix,
        grad_query.astype(jnp.bfloat16),
        grad_keys.astype(jnp.bfloat16),
        grad_values.astype(jnp.bfloat16),
    )


def backward(saved, output_cotangent, weights, vector_rows, decoder_segments, encoder_segments):
    runs = weight_runs(weights)
    width = weights.shape[0]
    tokens = saved["tokens"]
    encoder_rows = saved["encoder_rows"]
    unused, norm_back = jax.vjp(layer_norm, saved["resid_three"], vector_rows[4], vector_rows[5])
    grad_three, gain_three, shift_three = norm_back(
        output_cotangent.reshape(-1, width).astype(jnp.float32)
    )
    grad_low = grad_three.astype(jnp.bfloat16)
    grad_hidden = jnp.dot(grad_low, runs[9], preferred_element_type=jnp.float32)
    grad_down = transposed_times(grad_low, saved["hidden"])
    unused, gelu_back = jax.vjp(jax.nn.gelu, saved["up_values"])
    grad_up = gelu_back(grad_hidden)[0].astype(jnp.bfloat16)
    grad_upper = transposed_times(saved["normed_two_low"], grad_up)
    into_two = grad_three + gradient_sum(times_transposed(grad_up, runs[8]))
    unused, norm_back = jax.vjp(layer_norm, saved["resid_two"], vector_rows[2], vector_rows[3])
    grad_two, gain_two, shift_two = norm_back(into_two)
    cross_out, cross_query, cross_key, cross_value = attention_back(
        grad_two,
        saved["cross_context"],
        saved["cross_query"],
        saved["cross_key"],
        saved["cross_value"],
        saved["cross_logsum"],
        decoder_segments,
        encoder_segments,
        False,
        runs[7],
    )
    part_one = times_transposed(cross_query, runs[4])
    part_encoder = times_transposed(cross_key, runs[5]) + times_transposed(cross_value, runs[6])
    sum_one, encoder_gradient = (
        lax.psum(part_one.astype(jnp.bfloat16), "tensor").astype(jnp.float32),
        lax.psum(part_encoder.astype(jnp.bfloat16), "tensor").astype(jnp.float32),
    )
    unused, norm_back = jax.vjp(layer_norm, saved["resid_one"], vector_rows[0], vector_rows[1])
    grad_one, gain_one, shift_one = norm_back(grad_two + sum_one)
    self_out, self_query, self_key, self_value = attention_back(
        grad_one,
        saved["self_context"],
        saved["self_query"],
        saved["self_key"],
        saved["self_value"],
        saved["self_logsum"],
        decoder_segments,
        decoder_segments,
        True,
        runs[3],
    )
    part_input = (
        times_transposed(self_query, runs[0])
        + times_transposed(self_key, runs[1])
        + times_transposed(self_value, runs[2])
    )
    input_gradient = grad_one + gradient_sum(part_input)
    grad_weights = jnp.concatenate(
        [
            transposed_times(tokens, self_query),
            transposed_times(tokens, self_key),
            transposed_times(tokens, self_value),
            self_out,
            transposed_times(saved["normed_one_low"], cross_query),
            transposed_times(encoder_rows, cross_key),
            transposed_times(encoder_rows, cross_value),
            cross_out,
            grad_upper,
            grad_down,
        ],
        axis=1,
    )
    grad_vectors = jnp.stack([gain_one, shift_one, gain_two, shift_two, gain_three, shift_three])
    return (input_gradient, encoder_gradient, grad_weights, grad_vectors)


def orthonormal(matrix):
    norm_value = jnp.sqrt(jnp.sum(matrix * matrix, axis=(-2, -1), keepdims=True) + 1e-06)
    current = matrix / norm_value
    for repeat in range(newton_turns):
        gram = jnp.einsum("...ji,...jk->...ik", current, current, precision=PRECISE)
        current = 1.5 * current - 0.5 * jnp.einsum(
            "...ij,...jk->...ik", current, gram, precision=PRECISE
        )
    return current


def soap_step(gradient, weight, first, second, left, right, left_basis, right_basis):
    left_new = MOMENT_DECAY * left + (1.0 - MOMENT_DECAY) * jnp.einsum(
        "...ij,...kj->...ik", gradient, gradient, precision=PRECISE
    )
    right_new = MOMENT_DECAY * right + (1.0 - MOMENT_DECAY) * jnp.einsum(
        "...ji,...jk->...ik", gradient, gradient, precision=PRECISE
    )
    left_turn = orthonormal(
        jnp.einsum("...ij,...jk->...ik", left_new, left_basis, precision=PRECISE)
    )
    right_turn = orthonormal(
        jnp.einsum("...ij,...jk->...ik", right_new, right_basis, precision=PRECISE)
    )
    partway = jnp.einsum("...ji,...jk->...ik", left_turn, gradient, precision=PRECISE)
    turned = jnp.einsum("...ik,...kl->...il", partway, right_turn, precision=PRECISE)
    first_new = MOMENT_DECAY * first + (1.0 - MOMENT_DECAY) * turned
    second_new = MOMENT_DECAY * second + (1.0 - MOMENT_DECAY) * turned * turned
    correction = 1.0 - MOMENT_DECAY**STEP
    direction = first_new / correction / (jnp.sqrt(second_new / correction) + ADAM_EPS)
    partback = jnp.einsum("...ij,...jk->...ik", left_turn, direction, precision=PRECISE)
    backward_step = jnp.einsum("...ik,...lk->...il", partback, right_turn, precision=PRECISE)
    weight_new = weight * (1.0 - LEARN_RATE * WEIGHT_DECAY) - LEARN_RATE * backward_step
    return (weight_new, first_new, second_new, left_new, right_new, left_turn, right_turn)


def adam_vector(gradient, weight, first, second):
    first_new = MOMENT_DECAY * first + (1.0 - MOMENT_DECAY) * gradient
    second_new = MOMENT_DECAY * second + (1.0 - MOMENT_DECAY) * gradient * gradient
    correction = 1.0 - MOMENT_DECAY**STEP
    weight_new = weight - VECTOR_RATE * (first_new / correction) / (
        jnp.sqrt(second_new / correction) + ADAM_EPS
    )
    return (weight_new, first_new, second_new)


def per_device(
    decoder_input,
    encoder_states,
    decoder_segments,
    encoder_segments,
    output_cotangent,
    block_slots,
    master,
    first_moment,
    second_moment,
    row_statistics,
    column_statistics,
    row_basis,
    column_basis,
    vectors,
    vector_first,
    vector_second,
):
    gathered, vector_full = (
        lax.all_gather(master.astype(jnp.bfloat16), "dp", axis=1, tiled=True),
        lax.all_gather(vectors.astype(jnp.bfloat16), "dp", axis=1, tiled=True),
    )
    block_height = master.shape[2]
    width = decoder_input.shape[2]
    row_count = width // block_height
    block_total = block_slots.shape[0]
    column_count = block_total // row_count
    blocks = jnp.take(gathered[0], block_slots, axis=0)
    weights = (
        blocks.reshape(row_count, column_count, block_height, HD)
        .transpose(0, 2, 1, 3)
        .reshape(width, column_count * HD)
    )
    vector_rows = vector_full.astype(jnp.float32)
    first_pass = forward(
        decoder_input, encoder_states, decoder_segments, encoder_segments, weights, vector_rows
    )
    output = first_pass["output"]
    fenced = lax.optimization_barrier((output, decoder_input, encoder_states, weights))
    saved = forward(
        fenced[1], fenced[2], decoder_segments, encoder_segments, fenced[3], vector_rows
    )
    input_gradient, encoder_gradient, grad_weights, grad_vectors = backward(
        saved, output_cotangent, weights, vector_rows, decoder_segments, encoder_segments
    )
    grad_blocks = (
        grad_weights.reshape(row_count, block_height, column_count, HD)
        .transpose(0, 2, 1, 3)
        .reshape(block_total, block_height, HD)
    )
    inverse = (
        jnp.zeros((block_total,), jnp.int32)
        .at[block_slots]
        .set(jnp.arange(block_total, dtype=jnp.int32))
    )
    by_slot = jnp.take(grad_blocks, inverse, axis=0)
    owned_count = master.shape[1]
    vector_cols = vectors.shape[1]
    summed, vector_sum = lax.psum((by_slot, grad_vectors), "dp")
    owned = lax.dynamic_slice_in_dim(summed, lax.axis_index("dp") * owned_count, owned_count, 0)
    vector_owned = lax.dynamic_slice_in_dim(
        vector_sum, lax.axis_index("dp") * vector_cols, vector_cols, 1
    )
    updated = soap_step(
        owned,
        master[0],
        first_moment[0],
        second_moment[0],
        row_statistics[0],
        column_statistics[0],
        row_basis[0],
        column_basis[0],
    )
    vector_new = adam_vector(vector_owned, vectors, vector_first, vector_second)
    block_output = output.reshape(decoder_input.shape).astype(jnp.bfloat16)
    return (
        block_output,
        input_gradient.reshape(decoder_input.shape),
        encoder_gradient.reshape(encoder_states.shape),
        updated[0][None],
        updated[1][None],
        updated[2][None],
        updated[3][None],
        updated[4][None],
        updated[5][None],
        updated[6][None],
        vector_new[0],
        vector_new[1],
        vector_new[2],
    )


def solution(mesh):
    return jax.shard_map(
        per_device,
        mesh=mesh,
        in_specs=(
            P("dp", None, None),
            P("dp", None, None),
            P("dp", None),
            P("dp", None),
            P("dp", None, None),
            P(),
            P("tensor", "dp", None, None),
            P("tensor", "dp", None, None),
            P("tensor", "dp", None, None),
            P("tensor", "dp", None, None),
            P("tensor", "dp", None, None),
            P("tensor", "dp", None, None),
            P("tensor", "dp", None, None),
            P(None, "dp"),
            P(None, "dp"),
            P(None, "dp"),
        ),
        out_specs=(
            P("dp", None, None),
            P("dp", None, None),
            P("dp", None, None),
            P("tensor", "dp", None, None),
            P("tensor", "dp", None, None),
            P("tensor", "dp", None, None),
            P("tensor", "dp", None, None),
            P("tensor", "dp", None, None),
            P("tensor", "dp", None, None),
            P("tensor", "dp", None, None),
            P(None, "dp"),
            P(None, "dp"),
            P(None, "dp"),
        ),
        check_vma=False,
    )
```

profile of v0, /device:TPU:0, one launch (start us, length us, event | category | flops | bytes accessed | tf_op | source)
XLA Modules:
  0.0 957.6 jit_solution(11813243756870171284)
XLA Ops:
  10.8 79.4 %all-gather.3.cloned.1.call-done = bf16[1,256,128,64]{2,3,0,1:T(8,128)(2,1)} async-done(((bf16[1,16,128,64]{2,3,0,1:T(8,128)(2,1)}), bf16[1,256,128,64]{2,3,0,1:T(8,128)(2,1)}) %all-gather.3.cloned.1.call-update) | async-done | bytes 4194320 | tf_op jit(solution)/shard_map/all_gather | solution.py:455
  90.2 5.2 gather_fusion
  95.4 5.8 copy_select_fusion
  106.7 29.8 %while.131 = (s32[]{:T(128)}, bf16[2,512,256]{2,1,0:T(8,128)(2,1)}, s32[2]{0:T(128)S(1)}, s32[1024]{0:T(1024)S(1)}, bf16[1024,256]{0,1:T(8,128)(2,1)S(1)}, /*ind...) while((s32[]{:T(128)}, bf16[2,512,256]{2,1,0:T(8,128)(2,1)}, ...), condition=%wide.region_3.4_spmd, body=%wide.region_0.3_spmd.sunk | while | flops 551028224 | bytes 21002432 | solution.py:97
  108.7 7.2 fusion.428
  115.9 4.9 fusion.429
  123.6 7.2 fusion.428
  130.8 4.9 fusion.429
  136.6 2.5 convolution_convert_fusion.7
  139.2 38.6 %all-gather = bf16[16,32,6]{1,2,0:T(8,128)(2,1)S(1)} all-gather(bf16[1,32,6]{1,2,0:T(8,128)(2,1)S(1)} %convert_bitcast_fusion.2), channel_id=1, replica_groups=mesh['dp'=16,'tensor'=2] {'dp'}, dimensions={0}, use_global_device_ids=true | all-gather | bytes 6528 | tf_op jit(solution)/shard_map/all_gather | solution.py:456
  188.9 29.7 %while.132 = (s32[]{:T(128)}, bf16[2,512,256]{2,1,0:T(8,128)(2,1)}, s32[2]{0:T(128)S(1)}, s32[1024]{0:T(1024)S(1)}, s32[1024]{0:T(1024)S(1)}, /*index=5*/bf16[10...) while((s32[]{:T(128)}, bf16[2,512,256]{2,1,0:T(8,128)(2,1)}, ...), condition=%wide.region_10.11_spmd, body=%wide.region_7.10_spmd.sunk | while | flops 549979136 | bytes 21522628 | solution.py:97
  190.7 7.2 fusion.433
  197.9 4.9 fusion.434
  205.6 7.2 fusion.433
  212.8 4.9 fusion.434
  218.5 2.5 convolution_convert_fusion.6
  221.1 15.6 %all-reduce.14.cloned.1.call-done = bf16[1024,512]{1,0:T(8,128)(2,1)} async-done(((bf16[1024,512]{1,0:T(8,128)(2,1)}), bf16[1024,512]{1,0:T(8,128)(2,1)}) %all-reduce.14.cloned.1.call-update) | async-done | bytes 1048592 | tf_op jit(solution)/shard_map/psum | solution.py:45
  240.8 5.6 convolution_convert_fusion.5
  246.8 20.7 %all-reduce.16.cloned.1.call-done = bf16[1024,512]{1,0:T(8,128)(2,1)} async-done(((bf16[1024,512]{1,0:T(8,128)(2,1)}), bf16[1024,512]{1,0:T(8,128)(2,1)}) %all-reduce.16.cloned.1.call-update) | async-done | bytes 1048592 | tf_op jit(solution)/shard_map/psum | solution.py:45
  267.4 2.6 fusion.230
  278.2 22.9 %while.133 = (s32[]{:T(128)}, bf16[2,512,256]{2,1,0:T(8,128)(2,1)}, f32[2,4,512]{2,1,0:T(4,128)S(1)}, s32[2]{0:T(128)S(1)}, s32[1024]{0:T(1024)S(1)}, /*index=5*...) while((s32[]{:T(128)}, bf16[2,512,256]{2,1,0:T(8,128)(2,1)}, ...), condition=%wide.region_20.21_spmd, body=%wide.region_17.20_spmd.sunk | while | flops 563608064 | bytes 30488780 | solution.py:97
  285.2 3.6 fusion.441
  296.6 3.6 fusion.441
  301.1 2.7 convolution_convert_fusion.4
  308.0 16.8 %all-reduce.18.cloned.1.call-done = bf16[1024,512]{1,0:T(8,128)(2,1)} async-done(((bf16[1024,512]{1,0:T(8,128)(2,1)}), bf16[1024,512]{1,0:T(8,128)(2,1)}) %all-reduce.18.cloned.1.call-update) | async-done | bytes 1048592 | tf_op jit(solution)/shard_map/psum | solution.py:45
  331.8 22.4 %while.134 = (s32[]{:T(128)}, bf16[2,512,256]{2,1,0:T(8,128)(2,1)}, f32[2,4,512]{2,1,0:T(4,128)S(1)}, s32[2]{0:T(128)S(1)}, s32[1024]{0:T(1024)S(1)}, /*index=5*...) while((s32[]{:T(128)}, bf16[2,512,256]{2,1,0:T(8,128)(2,1)}, ...), condition=%wide.region_27.28_spmd, body=%wide.region_24.27_spmd.sunk | while | flops 562558976 | bytes 30484688 | solution.py:97
  338.5 3.6 fusion.447
  349.7 3.6 fusion.447
  354.2 2.5 convolution_convert_fusion.3
  356.8 20.9 %all-reduce.20.cloned.1.call-done = bf16[1024,512]{1,0:T(8,128)(2,1)} async-done(((bf16[1024,512]{1,0:T(8,128)(2,1)}), bf16[1024,512]{1,0:T(8,128)(2,1)}) %all-reduce.20.cloned.1.call-update) | async-done | bytes 1048592 | tf_op jit(solution)/shard_map/psum | solution.py:45
  377.7 2.6 fusion.229
  386.8 20.7 %all-reduce.22.cloned.1.call-done = bf16[1024,512]{1,0:T(8,128)(2,1)} async-done(((bf16[1024,512]{1,0:T(8,128)(2,1)}), bf16[1024,512]{1,0:T(8,128)(2,1)}) %all-reduce.22.cloned.1.call-update) | async-done | bytes 1048592 | tf_op jit(solution)/shard_map/psum | solution.py:45
  407.5 2.7 fusion.228
  414.3 3.6 fusion.67
  423.4 19.1 %all-reduce.24.cloned.1.call-done = bf16[1024,512]{1,0:T(8,128)(2,1)} async-done(((bf16[1024,512]{1,0:T(8,128)(2,1)}), bf16[1024,512]{1,0:T(8,128)(2,1)}) %all-reduce.24.cloned.1.call-update) | async-done | bytes 1048592 | tf_op jit(solution)/shard_map/psum | solution.py:49
  442.5 3.8 multiply_reduce_fusion.2
  452.2 39.6 %while.135 = (s32[]{:T(128)}, f32[1024,4,64]{0,2,1:T(8,128)}, f32[1024,4,64]{0,2,1:T(8,128)}, bf16[2,512,256]{2,1,0:T(8,128)(2,1)}, s32[2]{0:T(128)S(1)}, /*inde...) while((s32[]{:T(128)}, f32[1024,4,64]{0,2,1:T(8,128)}, ...), condition=%wide.region_41.42_spmd.clone, body=%wide.region_39.41_spmd.clone.sunk | while | flops 1375729664 | bytes 83167528 | solution.py:165
  457.2 3.6 fusion.460
  460.8 4.2 multiply_reduce_fusion.16
  476.5 4.6 fusion.460
  481.1 4.2 multiply_reduce_fusion.16
  491.9 2.6 convolution_convert_fusion
  502.9 12.5 %all-reduce.26.cloned.1.call-done = bf16[1024,512]{1,0:T(8,128)(2,1)} async-done(((bf16[1024,512]{1,0:T(8,128)(2,1)}), bf16[1024,512]{1,0:T(8,128)(2,1)}) %all-reduce.26.cloned.1.call-update) | async-done | bytes 1048592 | tf_op jit(solution)/shard_map/psum | solution.py:348
  515.5 3.5 multiply_reduce_fusion.3
  524.9 40.4 %while.136 = (s32[]{:T(128)}, f32[1024,4,64]{0,2,1:T(8,128)}, f32[1024,4,64]{0,2,1:T(8,128)}, bf16[2,512,256]{2,1,0:T(8,128)(2,1)}, s32[2]{0:T(128)S(1)}, /*inde...) while((s32[]{:T(128)}, f32[1024,4,64]{0,2,1:T(8,128)}, ...), condition=%wide.region_47.48_spmd.clone, body=%wide.region_45.47_spmd.clone.sunk | while | flops 1376778752 | bytes 83171616 | solution.py:165
  530.2 3.5 fusion.474
  533.8 4.2 multiply_reduce_fusion.17
  549.8 4.6 fusion.474
  554.4 4.2 multiply_reduce_fusion.17
  579.6 2.5 add_convert_fusion.1
  583.5 3.1 convolution_dynamic-update-slice_fusion.2
  586.6 4.5 convolution_dynamic-update-slice_fusion.1
  591.2 3.2 convolution_dynamic-update-slice_fusion
  594.4 9.2 copy.183
  603.6 9.9 %reshape.758 = f32[4,128,64,64]{1,0,3,2:T(4,128)} reshape(f32[512,4096]{0,1:T(8,128)} %copy.183) | data formatting | bytes 16777216 | tf_op jit(solution)/shard_map/reshape | solution.py:482
  613.5 7.8 copy.184
  621.3 7.8 gather_fusion.1
  629.1 6.0 broadcast_select_fusion
  636.6 3.0 fusion.372
  639.6 81.3 %psum.95 = f32[6,512]{1,0:T(8,128)S(1)} all-reduce(f32[6,512]{1,0:T(8,128)S(1)} %stack.2), channel_id=1, replica_groups=mesh['dp'=16,'tensor'=2] {'dp'}, use_global_device_ids=true, to_apply=%region_60.61 | all-reduce | flops 3072 | bytes 24576 | tf_op jit(solution)/shard_map/psum | solution.py:494
  721.6 2.9 reshape.757
  724.5 3.6 add_bitcast_fusion
  728.0 166.6 %all-reduce.28.cloned.1.call-done = f32[256,128,64]{1,2,0:T(8,128)} async-done(((f32[256,128,64]{1,2,0:T(8,128)}), f32[256,128,64]{1,2,0:T(8,128)}) %all-reduce.28.cloned.1.call-update) | async-done | bytes 8388624 | tf_op jit(solution)/shard_map/psum | solution.py:494
  911.5 3.2 fusion.99
  (480 shorter events, 230.7 us)
Async XLA Ops:
  7.2 171.3 %copy-start = (bf16[1,1024,512]{2,1,0:T(8,128)(2,1)S(1)}, bf16[1,1024,512]{2,1,0:T(8,128)(2,1)}, u32[]{:S(2)}) copy-start(bf16[1,1024,512]{2,1,0:T(8,128)(2,1)} %param.29) | copy-start | bytes 3145732
  7.2 83.0 %all-gather.3.cloned.1.call-start = ((), (), s32[]{:S(2)}) async-start(), calls=%async_computation | async-start | bytes 4456448 | tf_op jit(solution)/shard_map/all_gather | solution.py:455
  9.1 173.8 %all-reduce.12.cloned.1.call-start = ((), (), s32[]{:S(2)}) async-start(), calls=%async_computation.1 | async-start | bytes 2097152 | tf_op jit(solution)/shard_map/psum | solution.py:45
  10.8 84.7 %copy-start.85 = (s32[256]{0:T(256)}, s32[256]{0:T(256)S(1)}, u32[]{:S(2)}) copy-start(s32[256]{0:T(256)S(1)} %compare_select_fusion.1) | copy-start | bytes 3076
  102.0 4.7 copy-start.41
  106.7 32.4 %copy-start.75 = (f32[6,32]{1,0:T(8,128)S(1)}, f32[6,32]{1,0:T(8,128)}, u32[]{:S(2)}) copy-start(f32[6,32]{1,0:T(8,128)} %param.41) | copy-start | bytes 2308
  139.1 97.6 %all-reduce.14.cloned.1.call-start = ((), (), s32[]{:S(2)}) async-start(), calls=%async_computation.2 | async-start | bytes 2097152 | tf_op jit(solution)/shard_map/psum | solution.py:45
  178.5 89.0 %copy-start.58 = (f32[1,512]{1,0:T(1,128)}, f32[1,512]{1,0:T(1,128)S(1)}, u32[]{:S(2)}) copy-start(f32[1,512]{1,0:T(1,128)S(1)} %get-tuple-element.1039) | copy-start | bytes 6148
  178.5 89.0 %copy-start.69 = (f32[1,512]{1,0:T(1,128)}, f32[1,512]{1,0:T(1,128)S(1)}, u32[]{:S(2)}) copy-start(f32[1,512]{1,0:T(1,128)S(1)} %get-tuple-element.1038) | copy-start | bytes 6148
  178.5 199.2 %copy-start.72 = (f32[1,512]{1,0:T(1,128)}, f32[1,512]{1,0:T(1,128)S(1)}, u32[]{:S(2)}) copy-start(f32[1,512]{1,0:T(1,128)S(1)} %get-tuple-element.1040) | copy-start | bytes 6148
  184.6 4.3 copy-start.47
  221.1 46.4 %all-reduce.16.cloned.1.call-start = ((), (), s32[]{:S(2)}) async-start(), calls=%async_computation.3 | async-start | bytes 2097152 | tf_op jit(solution)/shard_map/psum | solution.py:45
  246.5 78.3 %all-reduce.18.cloned.1.call-start = ((), (), s32[]{:S(2)}) async-start(), calls=%async_computation.4 | async-start | bytes 2097152 | tf_op jit(solution)/shard_map/psum | solution.py:45
  270.1 7.4 copy-start.61
  301.1 25.3 %copy-start.2 = (bf16[1024,4,64]{0,2,1:T(8,128)(2,1)}, bf16[1024,4,64]{0,2,1:T(8,128)(2,1)S(1)}, u32[]{:S(2)}) copy-start(bf16[1024,4,64]{0,2,1:T(8,128)(2,1)S(1)} %get-tuple-element.1657) | copy-start | bytes 1572868
  301.1 25.3 %copy-start.52 = (f32[2,4,512]{2,1,0:T(4,128)}, f32[2,4,512]{2,1,0:T(4,128)S(1)}, u32[]{:S(2)}) copy-start(f32[2,4,512]{2,1,0:T(4,128)S(1)} %get-tuple-element.564) | copy-start | bytes 49156
  303.9 73.8 %all-reduce.20.cloned.1.call-start = ((), (), s32[]{:S(2)}) async-start(), calls=%async_computation.5 | async-start | bytes 2097152 | tf_op jit(solution)/shard_map/psum | solution.py:45
  356.7 24.0 %copy-start.59 = (f32[1,512]{1,0:T(1,128)S(1)}, f32[1,512]{1,0:T(1,128)}, u32[]{:S(2)}) copy-start(f32[1,512]{1,0:T(1,128)} %copy-done.58) | copy-start | bytes 6148
  356.7 24.0 %copy-start.70 = (f32[1,512]{1,0:T(1,128)S(1)}, f32[1,512]{1,0:T(1,128)}, u32[]{:S(2)}) copy-start(f32[1,512]{1,0:T(1,128)} %copy-done.69) | copy-start | bytes 6148
  356.8 50.7 %all-reduce.22.cloned.1.call-start = ((), (), s32[]{:S(2)}) async-start(), calls=%async_computation.6 | async-start | bytes 2097152 | tf_op jit(solution)/shard_map/psum | solution.py:45
  380.3 66.0 %copy-start.54 = (f32[1024]{0:T(1024)}, f32[1024]{0:T(1024)S(1)}, u32[]{:S(2)}) copy-start(f32[1024]{0:T(1024)S(1)} %broadcast_multiply_fusion.1) | copy-start | bytes 12292
  380.8 65.5 %copy-start.56 = (f32[1024]{0:T(1024)}, f32[1024]{0:T(1024)S(1)}, u32[]{:S(2)}) copy-start(f32[1024]{0:T(1024)S(1)} %fusion.202) | copy-start | bytes 12292
  386.5 24.1 %copy-start.67 = (f32[1,512]{1,0:T(1,128)S(1)}, f32[1,512]{1,0:T(1,128)}, u32[]{:S(2)}) copy-start(f32[1,512]{1,0:T(1,128)} %get-tuple-element.1036) | copy-start | bytes 6148
  386.5 55.9 %all-reduce.24.cloned.1.call-start = ((), (), s32[]{:S(2)}) async-start(), calls=%async_computation.7 | async-start | bytes 2097152 | tf_op jit(solution)/shard_map/psum | solution.py:49
  413.0 5.0 copy-start.20
  413.0 33.3 %copy-start.65 = (f32[1024]{0:T(1024)}, f32[1024]{0:T(1024)S(1)}, u32[]{:S(2)}) copy-start(f32[1024]{0:T(1024)S(1)} %negate_multiply_fusion.2) | copy-start | bytes 12292
  421.5 93.9 %all-reduce.26.cloned.1.call-start = ((), (), s32[]{:S(2)}) async-start(), calls=%async_computation.8 | async-start | bytes 2097152 | tf_op jit(solution)/shard_map/psum | solution.py:348
  494.5 227.0 %all-reduce.30.cloned.1.call-start = ((), (), s32[]{:S(2)}) async-start(), calls=%async_computation.10 | async-start | bytes 4194304 | tf_op jit(solution)/shard_map/psum | solution.py:49
  497.4 18.1 %copy-start.16 = (bf16[1024,512]{1,0:T(8,128)(2,1)S(1)}, bf16[1024,512]{1,0:T(8,128)(2,1)}, u32[]{:S(2)}) copy-start(bf16[1024,512]{1,0:T(8,128)(2,1)} %all-reduce.18.cloned.1.call-done) | copy-start | bytes 3145732
  500.5 18.5 %copy-start.64 = (f32[1024]{0:T(1024)S(1)}, f32[1024]{0:T(1024)}, u32[]{:S(2)}) copy-start(f32[1024]{0:T(1024)} %copy-done.63) | copy-start | bytes 12292
  519.0 5.8 copy-start.3
  519.1 5.8 copy-start.53
  569.4 5.6 copy-start.14
  569.4 5.6 copy-start.33
  572.3 4.2 copy-start.18
  572.3 4.2 copy-start.42
  582.1 4.5 copy-start.55
  582.1 4.5 copy-start.57
  582.1 4.5 copy-start.60
  582.1 4.5 copy-start.71
  582.1 312.5 %all-reduce.28.cloned.1.call-start = ((), (), s32[]{:S(2)}) async-start(), calls=%async_computation.9 | async-start | bytes 16777216 | tf_op jit(solution)/shard_map/psum | solution.py:494
  582.2 4.5 copy-start.91
  586.6 4.6 copy-start.22
  586.6 4.6 copy-start.66
  586.6 4.5 copy-start.89
  621.3 7.9 copy-start.86
  635.1 4.4 copy-start.77
  635.1 4.4 copy-start.78
  635.2 4.4 copy-start.79
  635.2 4.4 copy-start.80
  635.2 4.4 copy-start.81
  635.2 85.6 %copy-start.76 = (f32[6,32]{1,0:T(8,128)S(1)}, f32[6,32]{1,0:T(8,128)}, u32[]{:S(2)}) copy-start(f32[6,32]{1,0:T(8,128)} %param.41) | copy-start | bytes 2308
  635.2 85.6 %copy-start.83 = (f32[6,32]{1,0:T(8,128)S(1)}, f32[6,32]{1,0:T(8,128)}, u32[]{:S(2)}) copy-start(f32[6,32]{1,0:T(8,128)} %param.42) | copy-start | bytes 2308
  635.2 85.6 %copy-start.84 = (f32[6,32]{1,0:T(8,128)S(1)}, f32[6,32]{1,0:T(8,128)}, u32[]{:S(2)}) copy-start(f32[6,32]{1,0:T(8,128)} %param.43) | copy-start | bytes 2308
  721.6 173.0 %copy-start.50 = (f32[1,16,64,64]{3,2,1,0:T(8,128)S(1)}, f32[1,16,64,64]{3,2,1,0:T(8,128)}, u32[]{:S(2)}) copy-start(f32[1,16,64,64]{3,2,1,0:T(8,128)} %param.38) | copy-start | bytes 786436
  724.5 172.3 %copy-start.51 = (f32[1,16,64,64]{3,2,1,0:T(8,128)S(1)}, f32[1,16,64,64]{3,2,1,0:T(8,128)}, u32[]{:S(2)}) copy-start(f32[1,16,64,64]{3,2,1,0:T(8,128)} %param.40) | copy-start | bytes 786436
  907.2 4.3 copy-start.45
  908.1 6.6 copy-start.46
  911.5 37.9 %copy-start.32 = (f32[16,64,64]{2,1,0:T(8,128)}, f32[16,64,64]{2,1,0:T(8,128)S(1)}, u32[]{:S(2)}) copy-start(f32[16,64,64]{2,1,0:T(8,128)S(1)} %fusion.103) | copy-start | bytes 786436
  914.8 4.7 copy-start.38
  941.0 4.8 copy-start.48
  941.1 4.8 copy-start.49
  942.4 7.0 copy-start.37
  944.8 4.5 copy-start.44
  (43 other events, 101.6 us)
Sparse Core Ops, SparseCore 0:
  11.4 78.7 all-gather.2
  139.2 18.1 all-reduce.11
  221.2 15.4 all-reduce.13
  246.6 20.7 all-reduce.15
  304.0 20.7 all-reduce.17
  356.9 20.7 all-reduce.19
  386.7 20.7 all-reduce.21
  421.6 20.7 all-reduce.23
  494.6 20.7 all-reduce.25
  582.2 22.4 all-reduce.29
  635.3 259.2 all-reduce.27
where the time goes:
time: 969 us; the launch traced here: 958 us
  waiting for transfers between devices  372 us (38%)
  matrix products  256 us (26%)
  blocking collectives  120 us (12%)
  local copies, waits for them, and re-layouts  95.7 us (10%)
  other arithmetic  88.4 us (9%)
  between operations  15.5 us (2%)
    psum x1, waiting for transfers between devices, per_device(): summed, vector_sum = lax.psum((by_slot, grad_vectors), 'dp')  167 us
    psum x6, waiting for transfers between devices, branch_sum(): lax.psum(partial_value.astype(jnp.bfloat16), 'tensor').astype(jnp.float32)  94.7 us
    psum x1, blocking collectives, per_device(): summed, vector_sum = lax.psum((by_slot, grad_vectors), 'dp')  81.3 us
    all_gather x1, waiting for transfers between devices, per_device(): lax.all_gather(master.astype(jnp.bfloat16), 'dp', axis=1, tiled=True)  79.4 us
    all_gather x1, blocking collectives, per_device(): lax.all_gather(vectors.astype(jnp.bfloat16), 'dp', axis=1, tiled=True)  38.6 us
    dot_general x8, matrix products, one_block(): jnp.einsum('hqk,khe->qhe', chances, value_heads, preferred_element_type=j...  34.1 us
    dot_general x13, matrix products, times_transposed(): lax.dot_general(left, right, (((1,), (1,)), ((), ())), preferred_element_...  32.7 us
    sub x4, matrix products, one_block(): expons = jnp.exp(scores - highest)  28.9 us
  transfers between devices with their start and end apart: 11, of which 9 were waited for; matrix products, arithmetic and copies ran while one was open for 9% of the time, Pallas kernels for 0%

commit v1 on v0

v1 whole, which is shorter than its diff:
```python
import jax
import jax.numpy as jnp
from jax import lax
from jax.sharding import PartitionSpec as P

HD = 64
FF = 2048
STEP = 10

PRECISE = lax.Precision.HIGHEST
NEGATIVE = -1e30
EPS_NORM = 1e-05
MOMENT_DECAY = 0.5
LEARN_RATE = 0.04
WEIGHT_DECAY = 0.01
VECTOR_RATE = 0.25
ADAM_EPS = 1e-08
NEWTON_TURNS = 8
VECTOR_ROWS = 16
F32 = jnp.float32
BF16 = jnp.bfloat16


def nn(left, right):
    return lax.dot_general(left, right, (((1,), (0,)), ((), ())), preferred_element_type=F32)


def nt(left, right):
    return lax.dot_general(left, right, (((1,), (1,)), ((), ())), preferred_element_type=F32)


def tn(left, right):
    return lax.dot_general(left, right, (((0,), (0,)), ((), ())), preferred_element_type=F32)


def low(values):
    return values.astype(BF16)


def normalise(inputs):
    center = inputs - jnp.mean(inputs, axis=-1, keepdims=True)
    spread = jnp.mean(center * center, axis=-1, keepdims=True)
    inverse = lax.rsqrt(spread + EPS_NORM)
    return center * inverse, inverse


def normalise_back(grad, hat, inverse, gain):
    scaled = grad * gain
    inner = (
        scaled
        - jnp.mean(scaled, axis=-1, keepdims=True)
        - hat * jnp.mean(scaled * hat, axis=-1, keepdims=True)
    )
    return (
        inner * inverse,
        jnp.sum(grad * hat, axis=0, keepdims=True),
        jnp.sum(grad, axis=0, keepdims=True),
    )


def attend(queries, key_rows, values, allowed):
    heads = queries.shape[1] // HD
    q = queries.reshape(-1, heads, HD)
    k = key_rows.reshape(-1, heads, HD)
    v = values.reshape(-1, heads, HD)
    scores = jnp.einsum("qhe,khe->hqk", q, k, preferred_element_type=F32) * HD**-0.5
    scores = jnp.where(allowed[None], scores, NEGATIVE)
    expons = jnp.exp(scores - jnp.max(scores, axis=-1, keepdims=True))
    chances = expons / jnp.sum(expons, axis=-1, keepdims=True)
    context = jnp.einsum("hqk,khe->qhe", low(chances), v, preferred_element_type=F32)
    return low(context.reshape(queries.shape)), chances


def attend_back(queries, key_rows, values, chances, grad_context):
    heads = queries.shape[1] // HD
    q = queries.reshape(-1, heads, HD)
    k = key_rows.reshape(-1, heads, HD)
    v = values.reshape(-1, heads, HD)
    g = grad_context.reshape(-1, heads, HD)
    grad_chances = jnp.einsum("qhe,khe->hqk", g, v, preferred_element_type=F32)
    grad_values = jnp.einsum("hqk,qhe->khe", low(chances), g, preferred_element_type=F32)
    grad_scores = low(
        chances * (grad_chances - jnp.sum(grad_chances * chances, axis=-1, keepdims=True))
    )
    grad_query = jnp.einsum("hqk,khe->qhe", grad_scores, k, preferred_element_type=F32) * HD**-0.5
    grad_keys = jnp.einsum("hqk,qhe->khe", grad_scores, q, preferred_element_type=F32) * HD**-0.5
    return (
        low(grad_query.reshape(queries.shape)),
        low(grad_keys.reshape(key_rows.shape)),
        low(grad_values.reshape(values.shape)),
    )


def both(weights, number, width):
    rows = weights[:, number * width : (number + 1) * width]
    return rows.reshape(-1, weights.shape[2])


def orthonormal(matrix):
    norm_value = jnp.sqrt(jnp.sum(matrix * matrix, axis=(-2, -1), keepdims=True) + 1e-06)
    current = matrix / norm_value
    for _ in range(NEWTON_TURNS):
        gram = jnp.einsum("...ji,...jk->...ik", current, current, precision=PRECISE)
        current = 1.5 * current - 0.5 * jnp.einsum(
            "...ij,...jk->...ik", current, gram, precision=PRECISE
        )
    return current


def soap_step(gradient, weight, first, second, left, right, left_basis, right_basis):
    left_new = MOMENT_DECAY * left + (1.0 - MOMENT_DECAY) * jnp.einsum(
        "...ij,...kj->...ik", gradient, gradient, precision=PRECISE
    )
    right_new = MOMENT_DECAY * right + (1.0 - MOMENT_DECAY) * jnp.einsum(
        "...ji,...jk->...ik", gradient, gradient, precision=PRECISE
    )
    left_turn = orthonormal(
        jnp.einsum("...ij,...jk->...ik", left_new, left_basis, precision=PRECISE)
    )
    right_turn = orthonormal(
        jnp.einsum("...ij,...jk->...ik", right_new, right_basis, precision=PRECISE)
    )
    partway = jnp.einsum("...ji,...jk->...ik", left_turn, gradient, precision=PRECISE)
    turned = jnp.einsum("...ik,...kl->...il", partway, right_turn, precision=PRECISE)
    first_new = MOMENT_DECAY * first + (1.0 - MOMENT_DECAY) * turned
    second_new = MOMENT_DECAY * second + (1.0 - MOMENT_DECAY) * turned * turned
    correction = 1.0 - MOMENT_DECAY**STEP
    direction = first_new / correction / (jnp.sqrt(second_new / correction) + ADAM_EPS)
    partback = jnp.einsum("...ij,...jk->...ik", left_turn, direction, precision=PRECISE)
    backward_step = jnp.einsum("...ik,...lk->...il", partback, right_turn, precision=PRECISE)
    weight_new = weight * (1.0 - LEARN_RATE * WEIGHT_DECAY) - LEARN_RATE * backward_step
    return (weight_new, first_new, second_new, left_new, right_new, left_turn, right_turn)


def adam_vector(gradient, weight, first, second):
    first_new = MOMENT_DECAY * first + (1.0 - MOMENT_DECAY) * gradient
    second_new = MOMENT_DECAY * second + (1.0 - MOMENT_DECAY) * gradient * gradient
    correction = 1.0 - MOMENT_DECAY**STEP
    weight_new = weight - VECTOR_RATE * (first_new / correction) / (
        jnp.sqrt(second_new / correction) + ADAM_EPS
    )
    return (weight_new, first_new, second_new)


def own_rows(values, index, chunk):
    early = lax.dynamic_slice_in_dim(values, index * chunk, chunk, 0)
    late = lax.dynamic_slice_in_dim(values, (3 - index) * chunk, chunk, 0)
    return jnp.concatenate([early, late], axis=0)


def in_order(mine, other, index, chunk):
    inner = jnp.where(index == 0, other, mine)
    outer = jnp.where(index == 0, mine, other)
    return jnp.concatenate([outer[:chunk], inner, outer[chunk:]], axis=0)


def per_device(
    decoder_input,
    encoder_states,
    decoder_segments,
    encoder_segments,
    output_cotangent,
    block_slots,
    master,
    first_moment,
    second_moment,
    row_statistics,
    column_statistics,
    row_basis,
    column_basis,
    vectors,
    vector_first,
    vector_second,
):
    core = lax.axis_index("tensor")
    cores = lax.axis_size("tensor")
    rings = lax.axis_size("dp")
    swap = [(0, 1), (1, 0)]
    owned_count, block_height = master.shape[1], master.shape[2]
    vector_cols = vectors.shape[1]
    length, width = decoder_input.shape[1], decoder_input.shape[2]
    row_count = width // block_height
    block_total = block_slots.shape[0]
    column_count = block_total // row_count
    hidden_width = FF // cores
    head_width = (column_count * HD - 2 * hidden_width) // 8
    chunk = length // 4

    payload = low(master[0]).transpose(0, 2, 1).reshape(owned_count * HD, block_height)
    small = jnp.pad(
        low(vectors).reshape(-1), (0, VECTOR_ROWS * block_height - vectors.size)
    ).reshape(VECTOR_ROWS, block_height)
    gathered = lax.all_gather(
        jnp.concatenate([payload, small], axis=0), ("dp", "tensor"), axis=0, tiled=False
    )
    gathered = gathered.reshape(rings, cores, owned_count * HD + VECTOR_ROWS, block_height)
    vector_rows = (
        gathered[:, 0, owned_count * HD :]
        .reshape(rings, -1)[:, : vectors.size]
        .reshape(rings, 6, vector_cols)
        .transpose(1, 0, 2)
        .reshape(6, width)
        .astype(F32)
    )
    blocks = gathered[:, :, : owned_count * HD].reshape(
        rings, cores, owned_count, HD, block_height
    )
    blocks = blocks.transpose(1, 0, 2, 3, 4).reshape(cores, block_total, HD, block_height)
    blocks = jnp.take(blocks, block_slots, axis=1, mode="clip")
    weights = (
        blocks.reshape(cores, row_count, column_count, HD, block_height)
        .transpose(0, 2, 3, 1, 4)
        .reshape(cores, column_count * HD, width)
    )

    def kind(number):
        return both(weights, number, head_width)

    upper = weights[:, 8 * head_width : 8 * head_width + hidden_width].reshape(-1, width)
    lower = weights[:, 8 * head_width + hidden_width :].reshape(-1, width)

    tokens, encoder_rows = decoder_input[0], encoder_states[0]
    ids, encoder_ids = decoder_segments[0], encoder_segments[0]
    own_tokens = own_rows(tokens, core, chunk)
    own_ids = own_rows(ids, core, chunk)
    places = jnp.arange(length)
    own_places = own_rows(places, core, chunk)
    self_allowed = (own_ids[:, None] == ids[None, :]) & (places[None, :] <= own_places[:, None])
    cross_allowed = own_ids[:, None] == encoder_ids[None, :]
    sq = low(nt(own_tokens, kind(0)))
    sk = low(nt(tokens, kind(1)))
    sv = low(nt(tokens, kind(2)))
    self_context, self_chances = attend(sq, sk, sv, self_allowed)
    hat_one, inverse_one = normalise(own_tokens.astype(F32) + nn(self_context, kind(3)))
    y_one = hat_one * vector_rows[0] + vector_rows[1]
    y_one_low = low(y_one)
    cq = low(nt(y_one_low, kind(4)))
    ck = low(nt(encoder_rows, kind(5)))
    cv = low(nt(encoder_rows, kind(6)))
    cross_context, cross_chances = attend(cq, ck, cv, cross_allowed)
    hat_two, inverse_two = normalise(y_one + nn(cross_context, kind(7)))
    y_two = hat_two * vector_rows[2] + vector_rows[3]
    y_two_low = low(y_two)
    up_values = nt(y_two_low, upper)
    hidden, gelu_back = jax.vjp(jax.nn.gelu, up_values)
    hidden = low(hidden)
    hat_three, inverse_three = normalise(y_two + nn(hidden, lower))
    own_output = low(hat_three * vector_rows[4] + vector_rows[5])

    cotangent = own_rows(output_cotangent[0], core, chunk).astype(F32)
    grad_three, gain_three, shift_three = normalise_back(
        cotangent, hat_three, inverse_three, vector_rows[4]
    )
    grad_low = low(grad_three)
    grad_up = low(gelu_back(nt(grad_low, lower))[0])
    grad_lower = tn(hidden, grad_low)
    grad_upper = tn(grad_up, y_two_low)
    grad_two, gain_two, shift_two = normalise_back(
        grad_three + nn(grad_up, upper), hat_two, inverse_two, vector_rows[2]
    )
    grad_low = low(grad_two)
    grad_cross_out = tn(cross_context, grad_low)
    gq, gk, gv = attend_back(cq, ck, cv, cross_chances, low(nt(grad_low, kind(7))))
    grad_cross = [tn(gq, y_one_low), tn(gk, encoder_rows), tn(gv, encoder_rows), grad_cross_out]
    part_encoder = low(nn(gk, kind(5)) + nn(gv, kind(6)))
    grad_one, gain_one, shift_one = normalise_back(
        grad_two + nn(gq, kind(4)), hat_one, inverse_one, vector_rows[0]
    )
    grad_low = low(grad_one)
    grad_self_out = tn(self_context, grad_low)
    gq, gk, gv = attend_back(sq, sk, sv, self_chances, low(nt(grad_low, kind(3))))
    grad_self = [tn(gq, own_tokens), tn(gk, tokens), tn(gv, tokens), grad_self_out]
    own_input = grad_one + nn(gq, kind(0))
    part_input = low(nn(gk, kind(1)) + nn(gv, kind(2)))

    half_input, half_encoder, half_output, half_own = lax.ppermute(
        (part_input, part_encoder, own_output, low(own_input)), "tensor", swap
    )
    block_output = in_order(own_output, half_output, core, chunk)
    input_gradient = (
        in_order(own_input, half_own.astype(F32), core, chunk)
        + part_input.astype(F32)
        + half_input.astype(F32)
    )
    encoder_gradient = part_encoder.astype(F32) + half_encoder.astype(F32)

    parts = [part.reshape(cores, -1, width) for part in grad_self + grad_cross]
    parts += [grad_upper.reshape(cores, -1, width), grad_lower.reshape(cores, -1, width)]
    grad_weights = low(jnp.concatenate(parts, axis=1))
    grad_blocks = (
        grad_weights.reshape(cores, column_count, HD, row_count, block_height)
        .transpose(0, 3, 1, 2, 4)
        .reshape(cores, block_total, HD, block_height)
    )
    inverse = (
        jnp.zeros((block_total,), jnp.int32)
        .at[block_slots]
        .set(jnp.arange(block_total, dtype=jnp.int32))
    )
    by_slot = jnp.take(grad_blocks, inverse, axis=1, mode="clip")
    by_slot = by_slot.reshape(cores, rings, owned_count * HD, block_height)
    grad_vectors = jnp.concatenate(
        [gain_one, shift_one, gain_two, shift_two, gain_three, shift_three], axis=0
    )
    small = low(grad_vectors).reshape(6, rings, vector_cols).transpose(1, 0, 2).reshape(rings, -1)
    small = jnp.pad(small, ((0, 0), (0, VECTOR_ROWS * block_height - vectors.size)))
    small = jnp.broadcast_to(
        small.reshape(1, rings, VECTOR_ROWS, block_height),
        (cores, rings, VECTOR_ROWS, block_height),
    )
    terms = jnp.concatenate([by_slot, small], axis=2)
    mine = lax.dynamic_index_in_dim(terms, core, 0, False)
    sent = lax.dynamic_index_in_dim(terms, 1 - core, 0, False)
    arrived = lax.ppermute(sent, "tensor", swap)
    mine = low(mine.astype(F32) + arrived.astype(F32))
    summed = lax.psum_scatter(mine, "dp", scatter_dimension=0, tiled=True)[0].astype(F32)
    owned = summed[: owned_count * HD].reshape(owned_count, HD, block_height).transpose(0, 2, 1)
    vector_owned = summed[owned_count * HD :].reshape(-1)[: vectors.size].reshape(vectors.shape)

    updated = soap_step(
        owned,
        master[0],
        first_moment[0],
        second_moment[0],
        row_statistics[0],
        column_statistics[0],
        row_basis[0],
        column_basis[0],
    )
    vector_new = adam_vector(vector_owned, vectors, vector_first, vector_second)
    return (
        block_output[None],
        input_gradient[None],
        encoder_gradient[None],
        updated[0][None],
        updated[1][None],
        updated[2][None],
        updated[3][None],
        updated[4][None],
        updated[5][None],
        updated[6][None],
        vector_new[0],
        vector_new[1],
        vector_new[2],
    )


def solution(mesh):
    blocks = P("tensor", "dp", None, None)
    rows = P("dp", None, None)
    return jax.shard_map(
        per_device,
        mesh=mesh,
        in_specs=(rows, rows, P("dp", None), P("dp", None), rows, P())
        + (blocks,) * 7
        + (P(None, "dp"),) * 3,
        out_specs=(rows,) * 3 + (blocks,) * 7 + (P(None, "dp"),) * 3,
        check_vma=False,
    )
```

time: 969 us -> 522 us (0.54)
  waiting for transfers between devices: 372 us -> 157 us
  blocking collectives: 120 us -> 0 us
  matrix products: 256 us -> 178 us
  other arithmetic: 88.4 us -> 42 us
  local copies, waits for them, and re-layouts: 95.7 us -> 122 us
    psum x10 -> x0, waiting for transfers between devices: 293 us -> none  [the longest x1 167 us: per_device(): summed, vector_sum = lax.psum((by_slot, grad_vectors), 'dp')]
    psum x1 -> x0, blocking collectives: 81.3 us -> none  [per_device(): summed, vector_sum = lax.psum((by_slot, grad_vectors), 'dp')]
    reduce_scatter x0 -> x1, waiting for transfers between devices: none -> 76.2 us  [per_device(): lax.psum_scatter(mine, 'dp', scatter_dimension=0, tiled=True)[0].astype(F32)]
    dot_general x71 -> x40, matrix products: 172 us -> 106 us  [the longest x10 20.3 us: tn(): lax.dot_general(left, right, (((0,), (0,)), ((), ())), preferred_element_...]
    reduce_sum x23 -> x5, other arithmetic: 40.6 us -> 1.88 us  [the longest x1 1.33 us: normalise_back(): jnp.sum(grad * hat, axis=0, keepdims=True)]
    all_gather x1 -> x0, blocking collectives: 38.6 us -> none  [per_device(): lax.all_gather(vectors.astype(jnp.bfloat16), 'dp', axis=1, tiled=True)]
    reshape x1 -> x6, local copies, waits for them, and re-layouts: 9.9 us -> 34.4 us  [the longest x1 13.1 us: per_device(): weights = blocks.reshape(cores, row_count, column_count, HD, block_height...]
    gather x2 -> x3, local copies, waits for them, and re-layouts: 13.1 us -> 33.9 us  [the longest x2 21.7 us: per_device(): by_slot = jnp.take(grad_blocks, inverse, axis=1, mode='clip')]
  transfers between devices with their start and end apart: 11 -> 7, of which waited for: 9 -> 3; matrix products, arithmetic and copies ran while one was open for 9% -> 5% of each run, Pallas kernels for 0% -> 0%
where the time goes in v1:
time: 522 us; the launch traced here: 515 us
  matrix products  178 us (34%)
  waiting for transfers between devices  157 us (30%)
  local copies, waits for them, and re-layouts  122 us (23%)
  other arithmetic  42 us (8%)
  between operations  15.5 us (3%)
    reduce_scatter x1, waiting for transfers between devices, per_device(): lax.psum_scatter(mine, 'dp', scatter_dimension=0, tiled=True)[0].astype(F32)  76.2 us
    all_gather x1, waiting for transfers between devices, per_device(): lax.all_gather(jnp.concatenate([payload, small], axis=0), ('dp', 'tensor'...  73.4 us
    dot_general x16, matrix products, orthonormal(): gram = jnp.einsum('...ji,...jk->...ik', current, current, precision=PRECISE)  24.3 us
    convert_element_type x5, other arithmetic, low(): return values.astype(BF16)  22 us
    sub x2, matrix products, attend(): expons = jnp.exp(scores - jnp.max(scores, axis=-1, keepdims=True))  21.7 us
    gather x2, local copies, waits for them, and re-layouts, per_device(): by_slot = jnp.take(grad_blocks, inverse, axis=1, mode='clip')  21.7 us
    dot_general x10, matrix products, tn(): lax.dot_general(left, right, (((0,), (0,)), ((), ())), preferred_element_...  20.3 us
    dot_general x2, matrix products, attend(): jnp.einsum('hqk,khe->qhe', low(chances), v, preferred_element_type=F32)  17.9 us
  transfers between devices with their start and end apart: 7, of which 3 were waited for; matrix products, arithmetic and copies ran while one was open for 5% of the time, Pallas kernels for 0%

profile of v1, /device:TPU:0, one launch (start us, length us, event | category | flops | bytes accessed | tf_op | source)
XLA Modules:
  0.0 515.5 jit_solution(8930998057035857565)
XLA Ops:
  17.0 1.8 fusion.32
  18.8 73.4 %all-gather.3.cloned.1.call-done = bf16[33280,128]{1,0:T(8,128)(2,1)} async-done(((bf16[1040,128]{1,0:T(8,128)(2,1)}), bf16[33280,128]{1,0:T(8,128)(2,1)}) %all-gather.3.cloned.1.call-update) | async-done | bytes 8519696 | tf_op jit(solution)/shard_map/all_gather | solution.py:193
  93.1 7.5 %slice.136 = bf16[16,2,1024,128]{3,2,1,0:T(8,128)(2,1)} slice(bf16[16,2,1040,128]{3,2,1,0:T(8,128)(2,1)} %bitcast.361), slice={[0:16], [0:2], [0:1024], [0:128]} | slice | bytes 16777216 | tf_op jit(solution)/shard_map/slice | solution.py:205
  100.6 9.9 %copy.67 = bf16[16,2,16,64,128]{4,3,2,0,1:T(8,128)(2,1)} copy(bf16[16,2,16,64,128]{4,3,2,1,0:T(8,128)(2,1)} %bitcast.350) | data formatting | bytes 16777216 | tf_op jit(solution)/shard_map/reshape | solution.py:205
  110.5 12.2 %gather_fusion = bf16[256,2,64,128]{3,2,1,0:T(8,128)(2,1)} fusion(bf16[2,256,64,128]{3,2,1,0:T(8,128)(2,1)} %bitcast.347, s32[1024]{0:T(1024)S(1)} %get-tuple-element.128), kind=kCustom, calls=%fused_computation | custom fusion | bytes 16778240 | tf_op jit(solution)/shard_map/jit(_take)/gather | solution.py:209
  122.7 11.2 %copy.138 = bf16[2,4,64,64,128]{4,1,3,2,0:T(4,128)(2,1)} copy(bf16[2,4,64,64,128]{4,3,0,2,1:T(8,128)(2,1)} %bitcast.348) | data formatting | bytes 16777216 | tf_op jit(solution)/shard_map/reshape | solution.py:211
  133.9 13.1 %reshape.402 = bf16[2,4096,512]{2,1,0:T(8,128)(2,1)} reshape(bf16[2,64,64,4,128]{4,3,2,1,0:T(4,128)(2,1)} %bitcast.351) | data formatting | bytes 16777216 | tf_op jit(solution)/shard_map/reshape | solution.py:213
  147.0 3.9 fusion.150
  150.9 1.5 copy-done.1
  152.4 2.5 fusion.149
  155.6 2.9 convolution_convert_fusion.2
  158.5 2.8 convolution_convert_fusion.3
  161.3 1.7 convolution_convert_fusion.4
  163.1 1.7 convolution_convert_fusion.5
  165.3 10.9 %fusion.153 = (f32[8,512]{1,0:T(8,128)S(1)}, f32[8,512,1024]{2,1,0:T(8,128)}) fusion(pred[512,1024]{1,0:T(8,128)(4,1)} %get-tuple-element.103, bf16[512,8,64]{0,2,1:T(8,128)(2,1)S(1)} %bitcast.398, bf16[1024,8,64]{0,2,1:T(8,128)(2,1)} %bitcast.402), kind=kOutput, calls=%fused_computation.287 | convolution fusion | flops 553649152 | bytes 18890752 | tf_op jit(solution)/shard_map/sub | solution.py:68
  176.2 8.9 %fusion.53 = bf16[8,64,512]{2,1,0:T(8,128)(2,1)S(1)} fusion(bf16[1024,8,64]{0,2,1:T(8,128)(2,1)} %bitcast.440, f32[8,512,1024]{2,1,0:T(8,128)} %get-tuple-element.106, f32[8,512]{1,0:T(8,128)S(1)} %get-tuple-element.105), kind=kOutput, calls=%fused_computation.105 | convolution fusion | flops 545521664 | bytes 18366464 | tf_op jit(solution)/shard_map/hqk,khe->qhe/dot_general | solution.py:70
  186.5 10.9 %fusion.155 = (f32[8,512]{1,0:T(8,128)S(1)}, f32[8,512,1024]{2,1,0:T(8,128)}) fusion(pred[512,1024]{1,0:T(8,128)(4,1)} %get-tuple-element.104, bf16[512,8,64]{0,2,1:T(8,128)(2,1)S(1)} %bitcast.400, bf16[1024,8,64]{0,2,1:T(8,128)(2,1)} %bitcast.404), kind=kOutput, calls=%fused_computation.289 | convolution fusion | flops 553649152 | bytes 18890752 | tf_op jit(solution)/shard_map/sub | solution.py:68
  197.4 9.0 %fusion.56 = bf16[8,64,512]{2,1,0:T(8,128)(2,1)S(1)} fusion(bf16[1024,8,64]{0,2,1:T(8,128)(2,1)} %bitcast.442, f32[8,512,1024]{2,1,0:T(8,128)} %get-tuple-element.110, f32[8,512]{1,0:T(8,128)S(1)} %get-tuple-element.109), kind=kOutput, calls=%fused_computation.106 | convolution fusion | flops 545521664 | bytes 18366464 | tf_op jit(solution)/shard_map/hqk,khe->qhe/dot_general | solution.py:70
  207.2 1.5 fusion.140
  208.8 2.0 fusion.157
  212.3 4.5 fusion.21
  216.9 3.6 convolution_convert_fusion
  220.4 1.9 multiply_reduce_fusion.3
  222.4 2.8 convolution_convert_fusion.1
  226.8 2.7 fusion.36
  229.5 8.6 %multiply_reduce_fusion.1 = (f32[8,512]{1,0:T(8,128)S(1)}, f32[8,512,1024]{2,1,0:T(8,128)}) fusion(f32[8,512,1024]{2,1,0:T(8,128)S(1)} %bitcast.356, f32[8,512]{1,0:T(8,128)S(1)} %get-tuple-element.109, bf16[512,8,64]{0,2,1:T(8,128)(2,1)} %bitcast.422, bf16[1024,8,64]{0,2,1:T(8,128)(2,1)} %bitcast.443), kind=kOutput, calls=%fused_computation.8 | convolution fusion | flops 549449728 | bytes 35160064 | tf_op jit(solution)/shard_map/qhe,khe->hqk/dot_general | solution.py:80
  238.1 7.3 %multiply_convert_fusion.1 = bf16[8,512,1024]{2,1,0:T(8,128)(2,1)S(1)} fusion(f32[8,512,1024]{2,1,0:T(8,128)} %get-tuple-element.117, f32[8,512]{1,0:T(8,128)S(1)} %get-tuple-element.116, f32[8,512,1024]{2,1,0:T(8,128)S(1)} %bitcast.356, f32[8,512]{1,0:T(8,128)S(1)} %get-tuple-element.109), kind=kLoop, calls=%fused_computation.7 | loop fusion | flops 16777216 | bytes 41975808 | tf_op jit(solution)/shard_map/convert_element_type | solution.py:37
  245.5 4.9 fusion.51
  250.3 2.5 multiply_convert_fusion.3
  255.4 2.7 fusion.33
  258.1 8.6 %multiply_reduce_fusion = (f32[8,512]{1,0:T(8,128)S(1)}, f32[8,512,1024]{2,1,0:T(8,128)}) fusion(f32[8,512,1024]{2,1,0:T(8,128)S(1)} %bitcast.354, f32[8,512]{1,0:T(8,128)S(1)} %get-tuple-element.105, bf16[512,8,64]{0,2,1:T(8,128)(2,1)} %bitcast.424, bf16[1024,8,64]{0,2,1:T(8,128)(2,1)} %bitcast.441), kind=kOutput, calls=%fused_computation.6 | convolution fusion | flops 549449728 | bytes 35160064 | tf_op jit(solution)/shard_map/qhe,khe->hqk/dot_general | solution.py:80
  266.6 7.4 %multiply_convert_fusion = bf16[8,512,1024]{2,1,0:T(8,128)(2,1)S(1)} fusion(f32[8,512,1024]{2,1,0:T(8,128)} %get-tuple-element.120, f32[8,512]{1,0:T(8,128)S(1)} %get-tuple-element.119, f32[8,512,1024]{2,1,0:T(8,128)S(1)} %bitcast.354, f32[8,512]{1,0:T(8,128)S(1)} %get-tuple-element.105), kind=kLoop, calls=%fused_computation.5 | loop fusion | flops 16777216 | bytes 41975808 | tf_op jit(solution)/shard_map/convert_element_type | solution.py:37
  274.0 4.7 fusion.52
  278.8 1.6 multiply_convert_fusion.4
  281.0 2.6 fusion.59
  283.6 2.8 fusion.66
  286.5 1.5 fusion.65
  290.7 1.5 fusion.64
  292.2 1.5 fusion.63
  296.4 1.6 constant_dynamic-update-slice_fusion
  298.0 12.5 %convert_element_type.300 = bf16[2,64,64,4,128]{4,3,2,1,0:T(4,128)(2,1)} reshape(bf16[2,4096,512]{2,1,0:T(8,128)(2,1)} %constant_dynamic-update-slice_fusion) | data formatting | bytes 16777216 | tf_op jit(solution)/shard_map/convert_element_type | solution.py:37
  310.5 8.9 %copy.81 = bf16[2,4,64,64,128]{4,3,2,1,0:T(8,128)(2,1)} copy(bf16[2,4,64,64,128]{4,1,3,2,0:T(4,128)(2,1)} %bitcast.352) | data formatting | bytes 16777216 | tf_op jit(solution)/shard_map/transpose | solution.py:292
  319.4 12.5 %gather_fusion.1 = bf16[256,2,64,128]{3,2,1,0:T(8,128)(2,1)} fusion(bf16[2,256,64,128]{3,2,1,0:T(8,128)(2,1)} %bitcast.346, s32[1024]{0:T(1024)} %get-tuple-element.127), kind=kCustom, calls=%fused_computation.1 | custom fusion | bytes 16778240 | tf_op jit(solution)/shard_map/jit(_take)/gather | solution.py:300
  332.0 9.2 %copy.82 = bf16[2,256,64,128]{3,2,1,0:T(8,128)(2,1)} copy(bf16[2,256,64,128]{3,2,0,1:T(8,128)(2,1)} %bitcast.349) | data formatting | bytes 16777216 | tf_op jit(solution)/shard_map/jit(_take)/gather | solution.py:300
  341.1 4.5 fusion.12
  345.9 7.3 %collective-permute-done.4 = bf16[16,1040,128]{2,1,0:T(8,128)(2,1)} collective-permute-done((bf16[16,1040,128]{2,1,0:T(8,128)(2,1)}, bf16[16,1040,128]{2,1,0:T(8,128)(2,1)}, u32[]{:S(2)}, u32[]{:S(2)}) %collective-permute-start.4) | collective-permute-done | bytes 4259872 | tf_op jit(solution)/shard_map/ppermute | solution.py:314
  353.2 5.4 %fusion.4 = bf16[16,1040,128]{2,1,0:T(8,128)(2,1)} fusion(bf16[16,1040,128]{2,1,0:T(8,128)(2,1)} %collective-permute-done.4, s32[]{:T(128)S(6)} %select_n.61, bf16[2,16,1024,128]{3,2,1,0:T(8,128)(2,1)} %bitcast.345, bf16[2,16,16,128]{3,2,1,0:T(8,128)(2,1)S(1)} %broadcast_in_dim.107), kind=kLoop, calls=%fused_computation.18 | loop fusion | flops 17039360 | bytes 17039364 | tf_op jit(solution)/shard_map/convert_element_type | solution.py:37
  359.0 1.9 fusion.160
  361.0 2.9 add_convert_fusion
  366.5 1.7 add_convert_fusion.1
  371.4 2.1 fusion.31
  373.5 2.0 copy.102
  375.5 3.3 add_bitcast_fusion
  378.7 76.2 %reduce-scatter.2.cloned.1.call-done = bf16[1,1040,128]{2,1,0:T(8,128)(2,1)} async-done(((bf16[16,1040,128]{2,1,0:T(8,128)(2,1)}), bf16[1,1040,128]{2,1,0:T(8,128)(2,1)}) %reduce-scatter.2.cloned.1.call-update) | async-done | bytes 266256 | tf_op jit(solution)/shard_map/reduce_scatter | solution.py:316
  472.6 2.0 fusion.118
  476.0 1.9 fusion.161
  479.2 2.3 fusion.162
  482.9 1.9 fusion.163
  486.1 1.9 fusion.164
  489.4 1.9 fusion.165
  492.6 2.1 fusion.166
  496.0 1.9 fusion.167
  501.0 3.1 fusion.101
  505.3 2.5 fusion.68
  (292 shorter events, 63.3 us)
Async XLA Ops:
  7.2 148.4 %copy-start = (bf16[1,1024,512]{2,1,0:T(8,128)(2,1)S(1)}, bf16[1,1024,512]{2,1,0:T(8,128)(2,1)}, u32[]{:S(2)}) copy-start(bf16[1,1024,512]{2,1,0:T(8,128)(2,1)} %param.17) | copy-start | bytes 3145732
  7.2 7.7 %copy-start.66 = (s32[256]{0:T(256)S(1)}, s32[256]{0:T(256)}, u32[]{:S(2)}) copy-start(s32[256]{0:T(256)} %param.21) | copy-start | bytes 3076
  7.2 9.1 %copy-start.64 = (s32[1,1024]{1,0:T(1,128)S(1)}, s32[1,1024]{1,0:T(1,128)}, u32[]{:S(2)}) copy-start(s32[1,1024]{1,0:T(1,128)} %param.18) | copy-start | bytes 12292
  7.2 9.8 %copy-start.65 = (s32[1,1024]{1,0:T(1,128)S(1)}, s32[1,1024]{1,0:T(1,128)}, u32[]{:S(2)}) copy-start(s32[1,1024]{1,0:T(1,128)} %param.19) | copy-start | bytes 12292
  7.2 85.0 %all-gather.3.cloned.1.call-start = ((), (), s32[]{:S(2)}) async-start(), calls=%async_computation.2 | async-start | bytes 8785920 | tf_op jit(solution)/shard_map/all_gather | solution.py:193
  10.0 444.9 %reduce-scatter.2.cloned.1.call-start = ((), (), s32[]{:S(2)}) async-start(), calls=%async_computation.1 | async-start | bytes 4526080 | tf_op jit(solution)/shard_map/reduce_scatter | solution.py:316
  147.0 5.4 %copy-start.1 = (bf16[2,4096,512]{2,1,0:T(8,128)(2,1)S(1)}, bf16[2,4096,512]{2,1,0:T(8,128)(2,1)}, u32[]{:S(2)}) copy-start(bf16[2,4096,512]{2,1,0:T(8,128)(2,1)} %reshape.402) | copy-start | bytes 25165828
  152.4 8.9 %copy-start.17 = (bf16[2,256,512]{2,1,0:T(8,128)(2,1)}, bf16[2,256,512]{2,1,0:T(8,128)(2,1)S(1)}, u32[]{:S(2)}) copy-start(bf16[2,256,512]{2,1,0:T(8,128)(2,1)S(1)} %get-tuple-element.83) | copy-start | bytes 1572868
  152.4 10.7 %copy-start.15 = (bf16[2,256,512]{2,1,0:T(8,128)(2,1)}, bf16[2,256,512]{2,1,0:T(8,128)(2,1)S(1)}, u32[]{:S(2)}) copy-start(bf16[2,256,512]{2,1,0:T(8,128)(2,1)S(1)} %get-tuple-element.85) | copy-start | bytes 1572868
  152.4 12.4 %copy-start.19 = (bf16[2,256,512]{2,1,0:T(8,128)(2,1)}, bf16[2,256,512]{2,1,0:T(8,128)(2,1)S(1)}, u32[]{:S(2)}) copy-start(bf16[2,256,512]{2,1,0:T(8,128)(2,1)S(1)} %get-tuple-element.84) | copy-start | bytes 1572868
  152.4 54.0 %copy-start.11 = (bf16[2,256,512]{2,1,0:T(8,128)(2,1)}, bf16[2,256,512]{2,1,0:T(8,128)(2,1)S(1)}, u32[]{:S(2)}) copy-start(bf16[2,256,512]{2,1,0:T(8,128)(2,1)S(1)} %get-tuple-element.78) | copy-start | bytes 1572868
  155.6 5.7 %copy-start.56 = (bf16[1,1024,512]{2,1,0:T(8,128)(2,1)S(1)}, bf16[1,1024,512]{2,1,0:T(8,128)(2,1)}, u32[]{:S(2)}) copy-start(bf16[1,1024,512]{2,1,0:T(8,128)(2,1)} %param.16) | copy-start | bytes 3145732
  158.5 6.3 %copy-start.58 = (bf16[1,256,512]{1,2,0:T(8,128)(2,1)S(1)}, bf16[1,256,512]{1,2,0:T(8,128)(2,1)}, u32[]{:S(2)}) copy-start(bf16[1,256,512]{1,2,0:T(8,128)(2,1)} %copy.65) | copy-start | bytes 786436
  158.5 6.3 %copy-start.60 = (bf16[1,256,512]{1,2,0:T(8,128)(2,1)S(1)}, bf16[1,256,512]{1,2,0:T(8,128)(2,1)}, u32[]{:S(2)}) copy-start(bf16[1,256,512]{1,2,0:T(8,128)(2,1)} %copy.66) | copy-start | bytes 786436
  165.3 10.9 %copy-start.37 = (bf16[512,512]{0,1:T(8,128)(2,1)}, bf16[512,512]{0,1:T(8,128)(2,1)S(1)}, u32[]{:S(2)}) copy-start(bf16[512,512]{0,1:T(8,128)(2,1)S(1)} %convolution_convert_fusion.9) | copy-start | bytes 1572868
  176.1 9.0 %copy-start.30 = (bf16[2,256,512]{2,1,0:T(8,128)(2,1)S(1)}, bf16[2,256,512]{2,1,0:T(8,128)(2,1)}, u32[]{:S(2)}) copy-start(bf16[2,256,512]{2,1,0:T(8,128)(2,1)} %get-tuple-element.82) | copy-start | bytes 1572868
  176.2 9.0 %copy-start.59 = (bf16[1,256,512]{1,2,0:T(8,128)(2,1)S(1)}, bf16[1,256,512]{1,2,0:T(8,128)(2,1)}, u32[]{:S(2)}) copy-start(bf16[1,256,512]{1,2,0:T(8,128)(2,1)} %copy.65) | copy-start | bytes 786436
  176.2 9.0 %copy-start.61 = (bf16[1,256,512]{1,2,0:T(8,128)(2,1)S(1)}, bf16[1,256,512]{1,2,0:T(8,128)(2,1)}, u32[]{:S(2)}) copy-start(bf16[1,256,512]{1,2,0:T(8,128)(2,1)} %copy.66) | copy-start | bytes 786436
  176.2 9.8 %copy-start.21 = (bf16[2,256,512]{2,1,0:T(8,128)(2,1)S(1)}, bf16[2,256,512]{2,1,0:T(8,128)(2,1)}, u32[]{:S(2)}) copy-start(bf16[2,256,512]{2,1,0:T(8,128)(2,1)} %get-tuple-element.80) | copy-start | bytes 1572868
  185.7 20.8 %copy-start.4 = (f32[512,512]{0,1:T(8,128)}, f32[512,512]{0,1:T(8,128)S(1)}, u32[]{:S(2)}) copy-start(f32[512,512]{0,1:T(8,128)S(1)} %get-tuple-element.108) | copy-start | bytes 3145732
  186.5 10.9 %copy-start.39 = (bf16[512,512]{0,1:T(8,128)(2,1)}, bf16[512,512]{0,1:T(8,128)(2,1)S(1)}, u32[]{:S(2)}) copy-start(bf16[512,512]{0,1:T(8,128)(2,1)S(1)} %convolution_convert_fusion.8) | copy-start | bytes 1572868
  197.4 9.7 %copy-start.33 = (bf16[2,1024,512]{2,1,0:T(8,128)(2,1)S(1)}, bf16[2,1024,512]{2,1,0:T(8,128)(2,1)}, u32[]{:S(2)}) copy-start(bf16[2,1024,512]{2,1,0:T(8,128)(2,1)} %get-tuple-element.76) | copy-start | bytes 6291460
  216.8 9.9 %slice-start.4 = ((s8[16777216]{0:T(1024)(128)(4,1)}), s8[4194304]{0:T(1024)(128)(4,1)S(1)}, s32[]{:S(2)}) async-start(s8[16777216]{0:T(1024)(128)(4,1)} %bitcast.355), calls=%async_computation.7 | async-start | bytes 8388608
  216.9 9.9 %slice-start.5 = ((s8[16777216]{0:T(1024)(128)(4,1)}), s8[4194304]{0:T(1024)(128)(4,1)S(1)}, s32[]{:S(2)}) async-start(s8[16777216]{0:T(1024)(128)(4,1)} %bitcast.355), calls=%async_computation.8 | async-start | bytes 8388608
  220.4 6.3 %slice-start.6 = ((s8[16777216]{0:T(1024)(128)(4,1)}), s8[4194304]{0:T(1024)(128)(4,1)S(1)}, s32[]{:S(2)}) async-start(s8[16777216]{0:T(1024)(128)(4,1)} %bitcast.355), calls=%async_computation.9 | async-start | bytes 8388608
  222.4 4.4 slice-start.7
  225.5 27.4 %copy-start.2 = (f32[512,512]{0,1:T(8,128)}, f32[512,512]{0,1:T(8,128)S(1)}, u32[]{:S(2)}) copy-start(f32[512,512]{0,1:T(8,128)S(1)} %subtract_multiply_fusion.1) | copy-start | bytes 3145732
  245.4 4.9 copy-start.40
  245.4 9.9 %slice-start = ((s8[16777216]{0:T(1024)(128)(4,1)}), s8[4194304]{0:T(1024)(128)(4,1)S(1)}, s32[]{:S(2)}) async-start(s8[16777216]{0:T(1024)(128)(4,1)} %bitcast.353), calls=%async_computation.3 | async-start | bytes 8388608
  245.5 9.9 %slice-start.1 = ((s8[16777216]{0:T(1024)(128)(4,1)}), s8[4194304]{0:T(1024)(128)(4,1)S(1)}, s32[]{:S(2)}) async-start(s8[16777216]{0:T(1024)(128)(4,1)} %bitcast.353), calls=%async_computation.4 | async-start | bytes 8388608
  250.3 5.0 slice-start.2
  274.0 4.8 copy-start.38
  281.0 5.5 %copy-start.45 = (bf16[8,64,1024]{2,1,0:T(8,128)(2,1)S(1)}, bf16[8,64,1024]{2,1,0:T(8,128)(2,1)}, u32[]{:S(2)}) copy-start(bf16[8,64,1024]{2,1,0:T(8,128)(2,1)} %fusion.33) | copy-start | bytes 3145732
  281.0 5.5 %copy-start.57 = (bf16[1,1024,512]{2,1,0:T(8,128)(2,1)S(1)}, bf16[1,1024,512]{2,1,0:T(8,128)(2,1)}, u32[]{:S(2)}) copy-start(bf16[1,1024,512]{2,1,0:T(8,128)(2,1)} %param.16) | copy-start | bytes 3145732
  281.0 7.0 %copy-start.53 = (bf16[8,64,512]{2,1,0:T(8,128)(2,1)S(1)}, bf16[8,64,512]{2,1,0:T(8,128)(2,1)}, u32[]{:S(2)}) copy-start(bf16[8,64,512]{2,1,0:T(8,128)(2,1)} %copy-done.52) | copy-start | bytes 1572868
  283.6 5.6 %copy-start.6 = (f32[512,512]{0,1:T(8,128)S(1)}, f32[512,512]{0,1:T(8,128)}, u32[]{:S(2)}) copy-start(f32[512,512]{0,1:T(8,128)} %copy-done.4) | copy-start | bytes 3145732
  283.6 5.6 %copy-start.25 = (bf16[8,64,512]{2,1,0:T(8,128)(2,1)S(1)}, bf16[8,64,512]{2,1,0:T(8,128)(2,1)}, u32[]{:S(2)}) copy-start(bf16[8,64,512]{2,1,0:T(8,128)(2,1)} %fusion.51) | copy-start | bytes 1572868
  286.5 4.2 copy-start.7
  289.3 4.4 copy-start.3
  289.3 4.4 copy-start.36
  290.7 4.3 copy-start.28
  292.2 4.2 copy-start.27
  345.6 7.6 %collective-permute-start.4 = (bf16[16,1040,128]{2,1,0:T(8,128)(2,1)}, bf16[16,1040,128]{2,1,0:T(8,128)(2,1)}, u32[]{:S(2)}, u32[]{:S(2)}) collective-permute-start(bf16[16,1040,128]{2,1,0:T(8,128)(2,1)} %fusion.12), channel_id=1, source_target_pairs={{0,1},{1,0},{2,3},{3,2},{4,5},{5,4},{6,7},{7,6},{8,9},{9,8},{10,11... | collective-permute-start | bytes 12779528 | tf_op jit(solution)/shard_map/ppermute | solution.py:314
  358.7 5.5 %copy-start.20 = (bf16[2,256,512]{2,1,0:T(8,128)(2,1)S(1)}, bf16[2,256,512]{2,1,0:T(8,128)(2,1)}, u32[]{:S(2)}) copy-start(bf16[2,256,512]{2,1,0:T(8,128)(2,1)} %copy-done.19) | copy-start | bytes 1572868
  358.7 5.5 %copy-start.23 = (bf16[8,64,512]{2,1,0:T(8,128)(2,1)S(1)}, bf16[8,64,512]{2,1,0:T(8,128)(2,1)}, u32[]{:S(2)}) copy-start(bf16[8,64,512]{2,1,0:T(8,128)(2,1)} %fusion.52) | copy-start | bytes 1572868
  358.7 9.8 %collective-permute-start = (bf16[512,512]{0,1:T(8,128)(2,1)}, bf16[512,512]{0,1:T(8,128)(2,1)S(1)}, u32[]{:S(2)}, u32[]{:S(2)}) collective-permute-start(bf16[512,512]{0,1:T(8,128)(2,1)} %get-tuple-element.88), channel_id=1, source_target_pairs={{0,1},{1,0},{2,3},{3,2},{4,5},{5,4},{6,7},{7,6},{8,9},{9,8},{10,11... | collective-permute-start | bytes 1572872 | tf_op jit(solution)/shard_map/ppermute | solution.py:276
  361.0 4.7 copy-start.9
  361.0 4.7 copy-start.18
  363.9 11.6 %collective-permute-start.3 = (bf16[1024,512]{1,0:T(8,128)(2,1)}, bf16[1024,512]{1,0:T(8,128)(2,1)}, u32[]{:S(2)}, u32[]{:S(2)}) collective-permute-start(bf16[1024,512]{1,0:T(8,128)(2,1)} %add_convert_fusion), channel_id=1, source_target_pairs={{0,1},{1,0},{2,3},{3,2},{4,5},{5,4},{6,7},{7,6},{8,9},{9,8},{10,11... | collective-permute-start | bytes 3145736 | tf_op jit(solution)/shard_map/ppermute | solution.py:276
  365.4 4.6 collective-permute-start.1
  368.2 3.1 collective-permute-start.2
  375.4 80.4 %copy-start.48 = (f32[1,16,64,64]{3,2,1,0:T(8,128)S(1)}, f32[1,16,64,64]{3,2,1,0:T(8,128)}, u32[]{:S(2)}) copy-start(f32[1,16,64,64]{3,2,1,0:T(8,128)} %param.26) | copy-start | bytes 786436
  375.4 80.7 %copy-start.51 = (f32[1,16,64,64]{3,2,1,0:T(8,128)S(1)}, f32[1,16,64,64]{3,2,1,0:T(8,128)}, u32[]{:S(2)}) copy-start(f32[1,16,64,64]{3,2,1,0:T(8,128)} %param.28) | copy-start | bytes 786436
  466.6 4.3 copy-start.41
  470.9 34.4 %copy-start.10 = (f32[16,64,64]{2,1,0:T(8,128)}, f32[16,64,64]{2,1,0:T(8,128)S(1)}, u32[]{:S(2)}) copy-start(f32[16,64,64]{2,1,0:T(8,128)S(1)} %fusion.69) | copy-start | bytes 786436
  471.3 4.7 copy-start.14
  496.0 4.9 copy-start.49
  496.0 4.9 copy-start.50
  499.2 6.0 %copy-start.13 = (f32[16,128,128]{2,1,0:T(8,128)}, f32[16,128,128]{2,1,0:T(8,128)S(1)}, u32[]{:S(2)}) copy-start(f32[16,128,128]{2,1,0:T(8,128)S(1)} %fusion.39) | copy-start | bytes 3145732
  499.3 6.0 %slice-start.8 = ((bf16[1,1040,128]{2,1,0:T(8,128)(2,1)}), bf16[1,16,128]{2,1,0:T(8,128)(2,1)S(1)}, s32[]{:S(2)}) async-start(bf16[1,1040,128]{2,1,0:T(8,128)(2,1)} %reduce-scatter.2.cloned.1.call-done), calls=%async_computation.11 | async-start | bytes 8192 | tf_op jit(solution)/shard_map/slice | solution.py:318
  499.3 6.1 %copy-start.32 = (f32[1,16,128,64]{2,3,1,0:T(8,128)S(1)}, f32[1,16,128,64]{2,3,1,0:T(8,128)}, u32[]{:S(2)}) copy-start(f32[1,16,128,64]{2,3,1,0:T(8,128)} %param.22) | copy-start | bytes 1572868
  500.9 6.9 %copy-start.63 = (f32[6,32]{1,0:T(8,128)S(1)}, f32[6,32]{1,0:T(8,128)}, u32[]{:S(2)}) copy-start(f32[6,32]{1,0:T(8,128)} %param.29) | copy-start | bytes 2308
  500.9 6.9 %copy-start.67 = (f32[6,32]{1,0:T(8,128)S(1)}, f32[6,32]{1,0:T(8,128)}, u32[]{:S(2)}) copy-start(f32[6,32]{1,0:T(8,128)} %param.30) | copy-start | bytes 2308
  501.0 6.9 %copy-start.68 = (f32[6,32]{1,0:T(8,128)S(1)}, f32[6,32]{1,0:T(8,128)}, u32[]{:S(2)}) copy-start(f32[6,32]{1,0:T(8,128)} %param.31) | copy-start | bytes 2308
  (21 other events, 50.8 us)
Sparse Core Ops, SparseCore 0:
  11.5 80.7 all-gather.2
  358.8 96.0 reduce-scatter.1
